TPU v7x, 32 devices: a whole 2x2x4 slice. The times are simulated.
32 devices in a mesh: groups: 2 (over y), block: 4 (over x, core), tile: 4 (over z).
Axes of the slice: x: 2, y: 2, z: 4, core: 2. Of those that a mesh axis runs over, the one named last changes fastest.
Arguments:
- queries: float32 [8, 4, 16, 24, 1024], P(('groups', 'block'), 'tile'), parts along dimension 0
- keys: float32 [8, 4, 16, 24, 1024], P(('groups', 'block'), 'tile'), parts along dimension 0
- values: float32 [8, 4, 16, 24, 1024], P(('groups', 'block'), 'tile'), parts along dimension 0, may hold values from -6 to 6
- radii: int32 [4], replicated, may hold values from 1 to 4, as said below
Outputs:
- local_out: float32 [8, 4, 16, 24, 1024], P(('groups', 'block'), 'tile'), parts along dimension 0
- global_out: float32 [8, 4, 16, 24, 1024], P(('groups', 'block'), 'tile'), parts along dimension 0
There are 2 independent parts, one for each index of `groups`. A program takes and returns all parts, laid end to end along the dimension named above; an argument that names none is the same for every part. Nothing has to cross between parts.
Inputs may be any that keep to these rules, and one draw needn't show every extreme that they name: `radii`: every head's radius is at least 1 and some head has radius 4.
All inputs are finite; a program needn't handle non-finite values.
Results may differ from a plain program's by a relative error of at most 0.0003.
Values sent between devices are 32-bit elements; how exact they have to be, the bound alone decides.
A program may use at most 128 MiB of HBM per device.

v0:
```python
import math

import jax
import jax.numpy as jnp
from jax import lax
from jax.sharding import PartitionSpec as P

R_MAX = 4


def from_behind(value, axis, steps):
    count = lax.axis_size(axis)
    pairs = [(source, (source + steps) % count) for source in range(count)]
    return lax.ppermute(value, axis, pairs)


def entering(shard, axis, combine, identity):
    devices, mine = (lax.axis_size(axis), lax.axis_index(axis))
    everything = jax.tree.map(lambda part: lax.all_gather(part, axis), shard)
    start = jax.tree.map(
        lambda part, zero: jnp.broadcast_to(jnp.asarray(zero, part.dtype), part.shape),
        shard,
        identity,
    )

    def turn(k, before):
        reached = k < mine
        new = combine(before, jax.tree.map(lambda part: part[k], everything))
        return jax.tree.map(lambda a, b: jnp.where(reached, a, b), new, before)

    return lax.fori_loop(0, devices, turn, start)


def neighborhood(query_tile, key_tile, value_tile, radii, row_start, col_start, height, width):
    rows, cols, dim = query_tile.shape
    head_count = radii.shape[0]
    head_dim = dim // head_count
    key_h = key_tile.shape[0]
    key_w = key_tile.shape[1]
    row_margin = (key_h - rows) // 2
    col_margin = (key_w - cols) // 2
    query_rows = query_tile.reshape(rows * cols, head_count, head_dim)
    key_rows = key_tile.reshape(key_h * key_w, head_count, head_dim)
    value_rows = value_tile.reshape(key_h * key_w, head_count, head_dim)
    scores = jnp.einsum(
        "qhd,khd->hqk", query_rows, key_rows, precision=lax.Precision.HIGHEST
    ) / math.sqrt(head_dim)
    query_pos = jnp.arange(rows * cols, dtype=jnp.int32)
    key_pos = jnp.arange(key_h * key_w, dtype=jnp.int32)
    query_row = query_pos // cols
    query_col = query_pos % cols
    key_row = key_pos // key_w - row_margin
    key_col = key_pos % key_w - col_margin
    reach = jnp.maximum(
        jnp.abs(query_row[:, None] - key_row[None, :]),
        jnp.abs(query_col[:, None] - key_col[None, :]),
    )
    inside = (
        (col_start + key_col >= 0)
        & (col_start + key_col < width)
        & (row_start + key_row >= 0)
        & (row_start + key_row < height)
    )
    allowed = (reach[None, :, :] <= radii[:, None, None]) & inside[None, None, :]
    scores = jnp.where(allowed, scores, jnp.float32(-1e30))
    top = jnp.max(scores, axis=-1, keepdims=True)
    weights = jnp.exp(scores - top)
    weights = weights / jnp.sum(weights, axis=-1, keepdims=True)
    result = jnp.einsum("hqk,khd->qhd", weights, value_rows, precision=lax.Precision.HIGHEST)
    return result.reshape(rows, cols, dim)


def add_states(earlier, later):
    return jax.tree.map(lambda left, right: left + right, earlier, later)


def body(queries, keys, values, radii):
    rows, cols, dim = (queries.shape[2], queries.shape[3], queries.shape[4])
    head_count = radii.shape[0]
    head_dim = dim // head_count
    tile_count = lax.axis_size("tile")
    grid_cols = min(4, tile_count // 2)
    grid_rows = tile_count // grid_cols
    height = grid_rows * rows
    width = grid_cols * cols
    tile_here = lax.axis_index("tile")
    position = (tile_here + 1) % tile_count
    row_start = position // grid_cols * rows
    col_start = position % grid_cols * cols
    stacked = jnp.stack([keys[0, 0], values[0, 0]])
    side_parts = [
        from_behind(piece, "tile", by_step)
        for by_step, piece in ((1, stacked[:, :, cols - R_MAX :]), (-1, stacked[:, :, :R_MAX]))
    ]
    widened = jnp.concatenate([side_parts[0], stacked, side_parts[1]], axis=2)
    edge_parts = [
        from_behind(piece, "tile", by_step)
        for by_step, piece in (
            (grid_cols, widened[:, rows - R_MAX :]),
            (-grid_cols, widened[:, :R_MAX]),
        )
    ]
    padded = jnp.concatenate([edge_parts[0], widened, edge_parts[1]], axis=1)
    local_tile = neighborhood(
        queries[0, 0], padded[0], padded[1], radii, row_start, col_start, height, width
    )
    key_rows = keys[0, 0].reshape(rows * cols, head_count, head_dim)
    value_rows = values[0, 0].reshape(rows * cols, head_count, head_dim)
    feature = jax.nn.relu(key_rows)
    state = jnp.einsum("khd,khe->hde", feature, value_rows, precision=lax.Precision.HIGHEST)
    zsum = jnp.sum(feature, axis=0)
    vsum = jnp.sum(value_rows, axis=0)
    own = (state, zsum, vsum)
    zeros = jax.tree.map(jnp.zeros_like, own)
    earlier = entering(own, "block", add_states, zeros)
    full_state, full_z, full_v = lax.psum(add_states(earlier, own), "tile")
    count = ((lax.axis_index("block") + 1) * height * width).astype(jnp.float32)
    query_rows = jax.nn.relu(queries[0, 0].reshape(rows * cols, head_count, head_dim))
    numer = (
        jnp.einsum("qhd,hde->qhe", query_rows, full_state, precision=lax.Precision.HIGHEST)
        / math.sqrt(head_dim)
        + full_v[None, :, :]
    )
    denom = (
        jnp.einsum("qhd,hd->qh", query_rows, full_z, precision=lax.Precision.HIGHEST)
        / math.sqrt(head_dim)
        + count
    )
    global_tile = (numer / denom[:, :, None]).reshape(1, 1, rows, cols, dim)
    return (local_tile.reshape(1, 1, rows, cols, dim), global_tile)


def solution(mesh):
    return jax.shard_map(
        body,
        mesh=mesh,
        in_specs=(
            P(("groups", "block"), "tile", None, None, None),
            P(("groups", "block"), "tile", None, None, None),
            P(("groups", "block"), "tile", None, None, None),
            P(),
        ),
        out_specs=(
            P(("groups", "block"), "tile", None, None, None),
            P(("groups", "block"), "tile", None, None, None),
        ),
        check_vma=False,
    )
```

profile of v0, /device:TPU:19, one launch (start us, length us, event | category | flops | bytes accessed | tf_op | source)
XLA Modules:
  0.0 243.5 jit_solution(8093740516286024459)
XLA Ops:
  12.6 6.0 %fusion.14 = f32[4,256,256]{2,1,0:T(8,128)} fusion(f32[384,4,256]{2,1,0:T(4,128)} %reshape_squeeze.17, f32[384,4,256]{2,1,0:T(4,128)} %max.28), kind=kOutput, calls=%fused_computation.21 | convolution fusion | flops 1207959552 | bytes 4194304 | tf_op jit(solution)/shard_map/khd,khe->hde/dot_general | solution.py:110
  20.5 11.5 %collective-permute-done = f32[2,16,4,1024]{3,2,1,0:T(4,128)S(1)} collective-permute-done((f32[2,16,4,1024]{3,2,1,0:T(4,128)S(1)}, f32[2,16,4,1024]{3,2,1,0:T(4,128)S(1)}, u32[]{:S(2)}, u32[]{:S(2)}) %collective-permute-start) | collective-permute-done | bytes 524320 | tf_op jit(solution)/shard_map/ppermute | solution.py:14
  32.0 11.1 %collective-permute-done.1 = f32[2,16,4,1024]{3,2,1,0:T(4,128)S(1)} collective-permute-done((f32[2,16,4,1024]{3,2,1,0:T(4,128)S(1)}, f32[2,16,4,1024]{3,2,1,0:T(4,128)S(1)}, u32[]{:S(2)}, u32[]{:S(2)}) %collective-permute-start.1) | collective-permute-done | bytes 524320 | tf_op jit(solution)/shard_map/ppermute | solution.py:14
  47.4 2.9 %reshape_squeeze.16 = f32[384,4,256]{2,1,0:T(4,128)} reshape(f32[1,1,16,24,1024]{4,3,2,1,0:T(8,128)} %param.6) | data formatting | bytes 3145728 | tf_op jit(solution)/shard_map/reshape;squeeze | solution.py:42
  50.3 7.2 %all_gather.21 = f32[4,4,256]{2,1,0:T(4,128)S(1)} all-gather(f32[1,4,256]{2,1,0:T(4,128)S(1)} %all_gather.20), channel_id=1, replica_groups=mesh['groups'=2,'block'=4,'tile'=4] {'block'}, dimensions={0}, use_global_device_ids=true | all-gather | bytes 20480 | tf_op jit(solution)/shard_map/all_gather | solution.py:19
  57.4 5.3 %all_gather.23 = f32[4,4,256]{2,1,0:T(4,128)S(1)} all-gather(f32[1,4,256]{2,1,0:T(4,128)S(1)} %all_gather.22), channel_id=1, replica_groups=mesh['groups'=2,'block'=4,'tile'=4] {'block'}, dimensions={0}, use_global_device_ids=true | all-gather | bytes 20480 | tf_op jit(solution)/shard_map/all_gather | solution.py:19
  64.3 49.3 %collective-permute-done.2 = f32[2,4,32,1024]{3,2,1,0:T(8,128)} collective-permute-done((f32[2,4,32,1024]{3,2,1,0:T(8,128)}, f32[2,4,32,1024]{3,2,1,0:T(8,128)}, u32[]{:S(2)}, u32[]{:S(2)}) %collective-permute-start.2) | collective-permute-done | bytes 1048608 | tf_op jit(solution)/shard_map/ppermute | solution.py:14
  113.6 22.5 %collective-permute-done.3 = f32[2,4,32,1024]{3,2,1,0:T(8,128)} collective-permute-done((f32[2,4,32,1024]{3,2,1,0:T(8,128)}, f32[2,4,32,1024]{3,2,1,0:T(8,128)}, u32[]{:S(2)}, u32[]{:S(2)}) %collective-permute-start.3) | collective-permute-done | bytes 1048608 | tf_op jit(solution)/shard_map/ppermute | solution.py:14
  136.1 2.5 %pad_maximum_fusion = f32[2,24,32,1024]{3,2,1,0:T(8,128)S(1)} fusion(f32[2,4,32,1024]{3,2,1,0:T(8,128)} %collective-permute-done.3, f32[2,16,4,1024]{3,2,1,0:T(4,128)S(1)} %copy-done.8, f32[1,16,24,1024]{3,2,1,0:T(8,128)S(1)} %bitcast.50, f32[1,16,24,1024]{3,2,1,0:T(8,128)} %bitcast.51, f32[2,16,4,1024]{3,2,1,0:T(4,128)S(1)} %copy-done.6, ...), kind=kLoop, calls=%fused_computation.3 | loop fusion | flops 7864320 | bytes 12582912 | tf_op jit(solution)/shard_map/concatenate | solution.py:103
  138.6 3.3 %fusion.50 = (f32[1,24,32,1024]{3,2,1,0:T(8,128)}, f32[1,24,32,1024]{3,2,1,0:T(8,128)}) fusion(f32[2,24,32,1024]{3,2,1,0:T(8,128)S(1)} %pad_maximum_fusion), kind=kLoop, calls=%fused_computation.72 | loop fusion | bytes 12582912 | tf_op jit(solution)/shard_map/slice | solution.py:105
  141.9 5.1 %reshape_squeeze.15 = f32[768,4,256]{2,1,0:T(4,128)} reshape(f32[1,24,32,1024]{3,2,1,0:T(8,128)} %get-tuple-element.196) | data formatting | bytes 6291456 | tf_op jit(solution)/shard_map/reshape;squeeze | solution.py:43
  147.0 5.3 %reshape_squeeze.14 = f32[768,4,256]{2,1,0:T(4,128)} reshape(f32[1,24,32,1024]{3,2,1,0:T(8,128)} %get-tuple-element.195) | data formatting | bytes 6291456 | tf_op jit(solution)/shard_map/reshape;squeeze | solution.py:44
  152.3 8.8 %fusion.6 = (f32[4,384]{1,0:T(4,128)S(1)}, f32[4,768,384]{2,1,0:T(8,128)S(1)}) fusion(s32[384,768]{0,1:T(8,128)} %abs_maximum_fusion, s32[4]{0:T(128)S(1)} %copy-done.9, pred[768]{0:T(1024)(128)(4,1)S(1)} %compare_and_fusion, f32[384,4,256]{2,1,0:T(4,128)S(1)} %copy-done.3, f32[768,4,256]{2,1,0:T(4,128)} %reshape_squeeze.15), kind=kOutput, calls=%fused_computation.12 | convolution fusion | flops 3629775360 | bytes 10623760 | tf_op jit(solution)/shard_map/qhd,khd->hqk/dot_general | solution.py:45
  161.2 2.2 copy-done.1
  163.4 1.9 fusion.2
  165.3 6.5 %while.18 = (s32[]{:T(128)}, f32[4,256,256]{2,1,0:T(8,128)S(1)}, f32[4,256]{1,0:T(4,128)S(1)}, f32[4,256]{1,0:T(4,128)S(1)}, s32[]{:T(128)}, /*index=5*/f32[4,4,...) while((s32[]{:T(128)}, f32[4,256,256]{2,1,0:T(8,128)S(1)}, ...), condition=%wide.region_5.6_spmd.clone, body=%wide.region_4.5_spmd.clone.sunk | while | flops 792580 | bytes 3170435 | solution.py:31
  171.8 2.3 add.184
  174.2 14.4 %fusion.17 = f32[384,4,256]{0,2,1:T(8,128)} fusion(f32[4,768,384]{2,1,0:T(8,128)} %copy-done.1, f32[4,384]{1,0:T(4,128)S(1)} %fusion.2, f32[4,384]{1,0:T(4,128)S(1)} %get-tuple-element.203, s32[384,768]{0,1:T(8,128)} %abs_maximum_fusion, s32[4]{0:T(128)S(1)} %copy-done.9, pred[768]{0:T(1024)(128)(4,1)S(1)} %compare_and_fusion, ...), kind=kOutput, calls=%fused_computation.24 | convolution fusion | flops 3630956544 | bytes 10629904 | tf_op jit(solution)/shard_map/hqk,khd->qhd/dot_general | solution.py:69
  188.6 1.9 copy.29
  190.5 2.0 reshape_reshape.3
  192.4 10.0 %all-reduce = (f32[4,256]{1,0:T(4,128)S(1)}, f32[4,256]{1,0:T(4,128)S(1)}) all-reduce(f32[4,256]{1,0:T(4,128)S(1)} %add.189, f32[4,256]{1,0:T(4,128)S(1)} %add.185), channel_id=1, replica_groups=mesh['groups'=2,'block'=4,'tile'=4] {'tile'}, use_global_device_ids=true, to_apply=%region_8.9 | all-reduce | flops 2048 | bytes 16384 | tf_op jit(solution)/shard_map/psum | solution.py:116
  204.0 25.0 %all-reduce.3.cloned.1.call-done = f32[4,256,256]{2,1,0:T(8,128)} async-done(((f32[4,256,256]{2,1,0:T(8,128)}), f32[4,256,256]{2,1,0:T(8,128)}) %all-reduce.3.cloned.1.call-update) | async-done | bytes 1048592 | tf_op jit(solution)/shard_map/psum | solution.py:116
  229.0 4.9 %bitcast_divide_fusion = f32[384,4,256]{0,2,1:T(8,128)S(1)} fusion(f32[4,256,256]{2,1,0:T(8,128)} %all-reduce.3.cloned.1.call-done, f32[384,4,256]{2,1,0:T(4,128)S(1)} %copy-done.3, f32[384,4]{0,1:T(4,128)S(1)} %fusion.31, f32[4,256]{1,0:T(4,128)S(1)} %get-tuple-element.192), kind=kOutput, calls=%fused_computation.20 | convolution fusion | flops 1209532416 | bytes 4204544 | tf_op jit(solution)/shard_map/qhd,hde->qhe/dot_general | solution.py:120
  234.7 2.0 reshape.149
  (58 shorter events, 21.8 us)
Async XLA Ops:
  7.2 158.2 %all-gather.3.cloned.1.call-start = ((), (), s32[]{:S(2)}) async-start(), calls=%async_computation.1 | async-start | bytes 5242880 | tf_op jit(solution)/shard_map/all_gather | solution.py:19
  8.9 1.9 copy-start
  12.6 6.1 %copy-start.2 = (f32[1,1,16,24,1024]{4,3,2,1,0:T(8,128)S(1)}, f32[1,1,16,24,1024]{4,3,2,1,0:T(8,128)}, u32[]{:S(2)}) copy-start(f32[1,1,16,24,1024]{4,3,2,1,0:T(8,128)} %param.7) | copy-start | bytes 4718596
  18.6 210.4 %all-reduce.3.cloned.1.call-start = ((), (), s32[]{:S(2)}) async-start(), calls=%async_computation | async-start | bytes 2097152 | tf_op jit(solution)/shard_map/psum | solution.py:116
  18.9 13.0 %collective-permute-start = (f32[2,16,4,1024]{3,2,1,0:T(4,128)S(1)}, f32[2,16,4,1024]{3,2,1,0:T(4,128)S(1)}, u32[]{:S(2)}, u32[]{:S(2)}) collective-permute-start(f32[2,16,4,1024]{3,2,1,0:T(4,128)S(1)} %get-tuple-element.199), channel_id=1, source_target_pairs={{0,1},{1,2},{2,3},{3,0},{4,5},{5,6},{6,7},{7,4},{8,9},{9,10},{10,1... | collective-permute-start | bytes 1572872 | tf_op jit(solution)/shard_map/ppermute | solution.py:14
  20.3 22.8 %collective-permute-start.1 = (f32[2,16,4,1024]{3,2,1,0:T(4,128)S(1)}, f32[2,16,4,1024]{3,2,1,0:T(4,128)S(1)}, u32[]{:S(2)}, u32[]{:S(2)}) collective-permute-start(f32[2,16,4,1024]{3,2,1,0:T(4,128)S(1)} %get-tuple-element.200), channel_id=1, source_target_pairs={{0,3},{1,0},{2,1},{3,2},{4,7},{5,4},{6,5},{7,6},{8,11},{9,8},{10,9... | collective-permute-start | bytes 1572872 | tf_op jit(solution)/shard_map/ppermute | solution.py:14
  32.0 12.8 %copy-start.5 = (f32[2,16,4,1024]{3,2,1,0:T(4,128)}, f32[2,16,4,1024]{3,2,1,0:T(4,128)S(1)}, u32[]{:S(2)}) copy-start(f32[2,16,4,1024]{3,2,1,0:T(4,128)S(1)} %collective-permute-done) | copy-start | bytes 1572868
  43.0 1.8 copy-start.7
  44.8 68.8 %collective-permute-start.2 = (f32[2,4,32,1024]{3,2,1,0:T(8,128)}, f32[2,4,32,1024]{3,2,1,0:T(8,128)}, u32[]{:S(2)}, u32[]{:S(2)}) collective-permute-start(f32[2,4,32,1024]{3,2,1,0:T(8,128)} %get-tuple-element.197), channel_id=1, source_target_pairs={{0,2},{1,3},{2,0},{3,1},{4,6},{5,7},{6,4},{7,5},{8,10},{9,11},{10,... | collective-permute-start | bytes 3145736 | tf_op jit(solution)/shard_map/ppermute | solution.py:14
  46.7 89.4 %collective-permute-start.3 = (f32[2,4,32,1024]{3,2,1,0:T(8,128)}, f32[2,4,32,1024]{3,2,1,0:T(8,128)}, u32[]{:S(2)}, u32[]{:S(2)}) collective-permute-start(f32[2,4,32,1024]{3,2,1,0:T(8,128)} %get-tuple-element.198), channel_id=1, source_target_pairs={{0,2},{1,3},{2,0},{3,1},{4,6},{5,7},{6,4},{7,5},{8,10},{9,11},{10,... | collective-permute-start | bytes 3145736 | tf_op jit(solution)/shard_map/ppermute | solution.py:14
  47.3 88.7 %copy-start.6 = (f32[2,16,4,1024]{3,2,1,0:T(4,128)S(1)}, f32[2,16,4,1024]{3,2,1,0:T(4,128)}, u32[]{:S(2)}) copy-start(f32[2,16,4,1024]{3,2,1,0:T(4,128)} %copy-done.5) | copy-start | bytes 1572868
  50.3 85.8 %copy-start.8 = (f32[2,16,4,1024]{3,2,1,0:T(4,128)S(1)}, f32[2,16,4,1024]{3,2,1,0:T(4,128)}, u32[]{:S(2)}) copy-start(f32[2,16,4,1024]{3,2,1,0:T(4,128)} %copy-done.7) | copy-start | bytes 1572868
  147.0 5.3 %copy-start.3 = (f32[384,4,256]{2,1,0:T(4,128)S(1)}, f32[384,4,256]{2,1,0:T(4,128)}, u32[]{:S(2)}) copy-start(f32[384,4,256]{2,1,0:T(4,128)} %reshape_squeeze.16) | copy-start | bytes 4718596
  147.0 5.3 %copy-start.9 = (s32[4]{0:T(128)S(1)}, s32[4]{0:T(128)}, u32[]{:S(2)}) copy-start(s32[4]{0:T(128)} %param.9) | copy-start | bytes 52
  152.3 11.1 %copy-start.4 = (s32[384,768]{0,1:T(8,128)S(1)}, s32[384,768]{0,1:T(8,128)}, u32[]{:S(2)}) copy-start(s32[384,768]{0,1:T(8,128)} %abs_maximum_fusion) | copy-start | bytes 3538948
  161.2 2.2 copy-start.1
Sparse Core Ops, SparseCore 0:
  18.7 35.0 all-gather.2
  174.3 54.6 all-reduce.2
where the time goes:
time: 246 us; the launch traced here: 244 us
  waiting for transfers between devices  119 us (48%)
  matrix products  35.6 us (14%)
  local copies, waits for them, and re-layouts  29.3 us (12%)
  blocking collectives  22.6 us (9%)
  other arithmetic  18.4 us (7%)
  between operations  14.2 us (6%)
  starting transfers between devices  3.96 us (2%)
    ppermute x4, waiting for transfers between devices, from_behind(): return lax.ppermute(value, axis, pairs)  94.4 us
    psum x1, waiting for transfers between devices, body(): full_state, full_z, full_v = lax.psum(add_states(earlier, own), 'tile')  25 us
    dot_general x1, matrix products, neighborhood(): jnp.einsum('hqk,khd->qhd', weights, value_rows, precision=lax.Precision.H...  14.4 us
    all_gather x2, blocking collectives, entering(): everything = jax.tree.map(lambda part: lax.all_gather(part, axis), shard)  12.5 us
    psum x1, blocking collectives, body(): full_state, full_z, full_v = lax.psum(add_states(earlier, own), 'tile')  10 us
    dot_general x1, matrix products, neighborhood(): jnp.einsum('qhd,khd->hqk', query_rows, key_rows, precision=lax.Precision....  8.85 us
    select_n x8, other arithmetic, turn(): return jax.tree.map(lambda a, b: jnp.where(reached, a, b), new, before)  6.36 us
    dot_general x1, matrix products, body(): jnp.einsum('khd,khe->hde', feature, value_rows, precision=lax.Precision.H...  5.99 us
  transfers between devices with their start and end apart: 6, of which 5 were waited for; matrix products, arithmetic and copies ran while one was open for 22% of the time, Pallas kernels for 0%

commit v1 on v0

v1 whole, which is shorter than its diff:
```python
import functools
import math

import jax
import jax.numpy as jnp
from jax import lax
from jax.experimental import pallas as pl
from jax.experimental.pallas import tpu as pltpu
from jax.sharding import PartitionSpec as P

R_MAX = 4
FAR = 1e6
EXCLUDED = -1e30
MESH = pl.DeviceIdType.MESH


def split(x):
    high = x.astype(jnp.bfloat16)
    low = (x - high.astype(jnp.float32)).astype(jnp.bfloat16)
    return high, low


def dot3(a, b, over):
    def one(x, y):
        return lax.dot_general(x, y, (over, ((), ())), preferred_element_type=jnp.float32)

    return one(a[0], b[0]) + (one(a[0], b[1]) + one(a[1], b[0]))


def pick(side, after, before):
    if isinstance(side, int):
        return after if side > 0 else before
    return jnp.where(side > 0, after, before)


def guarded(when, act):
    if when is True:
        act()
    else:
        pl.when(when)(act)


def sides_of(count, here):
    if count == 1:
        return []
    if count == 2:
        return [(1 - 2 * here, True, 0)]
    return [(-1, here > 0, 1), (1, here < count - 1, 0)]


def strip_plan(rows, cols, grid_rows, grid_cols, grid_row, grid_col):
    down, across = sides_of(grid_rows, grid_row), sides_of(grid_cols, grid_col)
    raw, place, offset = [], {}, 0
    kinds = (
        [(None, j) for j in range(len(across))]
        + [(i, None) for i in range(len(down))]
        + [(i, j) for i in range(len(down)) for j in range(len(across))]
    )
    for i, j in kinds:
        tokens = (rows if i is None else R_MAX) * (cols if j is None else R_MAX)
        place[(i, j)] = offset
        raw.append((i, j, offset, tokens))
        offset += tokens
    strips = []
    for i, j, start, tokens in raw:
        dn = (0, True, None) if i is None else down[i]
        ac = (0, True, None) if j is None else across[j]
        if dn[1] is True:
            there = ac[1]
        elif ac[1] is True:
            there = dn[1]
        else:
            there = jnp.logical_and(dn[1], ac[1])
        opposite = place[(None if i is None else dn[2], None if j is None else ac[2])]
        strips.append((None if i is None else dn[0], None if j is None else ac[0], there, start, tokens, opposite))
    return strips, offset


def kernel(sizes, radii, q, k, v, local, glob, halo, send, near, far, acc, top, total, state, full,
           first, chain, passed, others, halo_send, halo_recv, step_send, step_recv, cross_send, cross_recv):
    frames, tiles, grid_rows, grid_cols, rows, cols, heads, width = sizes
    tokens = rows * cols
    half = heads // 2
    frame, tile = lax.axis_index("block"), lax.axis_index("tile")
    position = lax.rem(tile + 1, tiles)
    grid_row, grid_col = position // grid_cols, lax.rem(position, grid_cols)
    strips, used = strip_plan(rows, cols, grid_rows, grid_cols, grid_row, grid_col)
    padded = halo.shape[2]
    parity, couple = lax.rem(tile, 2), tile // 2
    peer = tile + 1 - 2 * parity
    couples = tiles // 2
    scale = 1.0 / math.sqrt(width)

    def neighbor(strip):
        r = grid_row + (0 if strip[0] is None else strip[0])
        c = grid_col + (0 if strip[1] is None else strip[1])
        return lax.rem(r * grid_cols + c + tiles - 1, tiles)

    def alike(d):
        return lax.rem(couple + d, couples) * 2 + parity

    if grid_rows == 2 and grid_cols == 2:
        if padded > used:
            halo[:, :, pl.ds(used, padded - used), :] = jnp.zeros((heads, 2, padded - used, width), jnp.float32)
    else:
        halo[...] = jnp.zeros_like(halo)

    barrier = pltpu.get_barrier_semaphore()

    def greet(axis, device):
        pl.semaphore_signal(barrier, inc=1, device_id={axis: device}, device_id_type=MESH)

    meetings = [(strip[2], "tile", neighbor(strip)) for strip in strips]
    if not (grid_rows == 2 and grid_cols == 2):
        meetings += [(True, "tile", peer)] + [(True, "tile", alike(d)) for d in range(1, couples)]
    meetings += [(frame > 0, "block", frame - 1), (frame < frames - 1, "block", frame + 1)]
    for there, axis, device in meetings:
        guarded(there, functools.partial(greet, axis, device))

    for part, x in enumerate((k, v)):
        for down, across, there, start, count, _ in strips:
            if down is None:
                for r in range(rows):
                    strip = pick(across, x[r * cols + cols - R_MAX:(r + 1) * cols, :], x[r * cols:r * cols + R_MAX, :])
                    for h in range(heads):
                        send[h, part, start + r * R_MAX:start + (r + 1) * R_MAX, :] = strip[:, h * width:(h + 1) * width]
                continue
            begin = pick(down, tokens - R_MAX * cols, 0)
            begin = begin if isinstance(begin, int) else pl.multiple_of(begin, cols)
            block = x[pl.ds(begin, R_MAX * cols), :]
            if across is None:
                for h in range(heads):
                    send[h, part, start:start + count, :] = block[:, h * width:(h + 1) * width]
                continue
            for r in range(R_MAX):
                row = block[r * cols:(r + 1) * cols]
                strip = pick(across, row[cols - R_MAX:], row[:R_MAX])
                for h in range(heads):
                    send[h, part, start + r * R_MAX:start + (r + 1) * R_MAX, :] = strip[:, h * width:(h + 1) * width]

    present = sum(1 if there is True else jnp.where(there, 1, 0) for there, _, _ in meetings)
    pl.semaphore_wait(barrier, present)

    def halo_copy(place, h):
        strip = strips[place]
        return pltpu.make_async_remote_copy(
            src_ref=send.at[h, :, pl.ds(strip[3], strip[4]), :],
            dst_ref=halo.at[h, :, pl.ds(strip[5], strip[4]), :],
            send_sem=halo_send.at[place, h],
            recv_sem=halo_recv.at[place, h],
            device_id={"tile": neighbor(strip)},
            device_id_type=MESH,
        )

    def halo_arrival(place, h):
        strip = strips[place]
        return pltpu.make_async_remote_copy(
            src_ref=send.at[h, :, pl.ds(strip[3], strip[4]), :],
            dst_ref=halo.at[h, :, pl.ds(strip[3], strip[4]), :],
            send_sem=halo_send.at[place, h],
            recv_sem=halo_recv.at[opposite_place[place], h],
            device_id={"tile": neighbor(strip)},
            device_id_type=MESH,
        )

    opposite_place = [[s[3] for s in strips].index(strip[5]) for strip in strips]

    def send_halo(h):
        for place, strip in enumerate(strips):
            guarded(strip[2], lambda place=place: halo_copy(place, h).start())

    def await_halo(h):
        for place, strip in enumerate(strips):
            guarded(strip[2], lambda place=place: halo_arrival(place, h).wait_recv())

    def lanes(h):
        return pl.ds(pl.multiple_of(h * width, width), width)

    def to_peer():
        return pltpu.make_async_remote_copy(
            src_ref=state.at[pl.ds((1 - parity) * half, half)], dst_ref=first,
            send_sem=step_send.at[0], recv_sem=step_recv.at[0],
            device_id={"tile": peer}, device_id_type=MESH)

    def to_next():
        return pltpu.make_async_remote_copy(
            src_ref=passed, dst_ref=chain,
            send_sem=step_send.at[1], recv_sem=step_recv.at[1],
            device_id={"block": frame + 1}, device_id_type=MESH)

    def to_alike(d):
        return pltpu.make_async_remote_copy(
            src_ref=passed, dst_ref=others.at[d - 1],
            send_sem=cross_send.at[d - 1], recv_sem=cross_recv.at[d - 1],
            device_id={"tile": alike(d)}, device_id_type=MESH)

    def hand_back():
        return pltpu.make_async_remote_copy(
            src_ref=full.at[pl.ds(parity * half, half)], dst_ref=full.at[pl.ds(parity * half, half)],
            send_sem=step_send.at[2], recv_sem=step_recv.at[2],
            device_id={"tile": peer}, device_id_type=MESH)

    send_halo(0)

    def one_state(h, _):
        feature = jnp.maximum(k[:, lanes(h)], 0.0)
        value = v[:, lanes(h)]
        state[h, 0:width, :] = dot3(split(feature), split(value), ((0,), (0,)))
        line = lax.broadcasted_iota(jnp.int32, (8, width), 0)
        zsum = jnp.sum(feature, axis=0, keepdims=True)
        vsum = jnp.sum(value, axis=0, keepdims=True)
        state[h, width:width + 8, :] = jnp.where(line == 0, zsum, jnp.where(line == 1, vsum, 0.0))
        return 0

    lax.fori_loop(0, heads, one_state, 0)
    to_peer().start()
    send_halo(1)

    def over(count_, axis, shape, per):
        index = lax.broadcasted_iota(jnp.int32, shape, axis).astype(jnp.float32)
        major = jnp.floor((index + 0.5) * (1.0 / per))
        return index, major, index - major * per

    _, q_row, q_col = over(tokens, 0, (tokens, 1), cols)
    _, k_row, k_col = over(tokens, 1, (1, tokens), cols)
    near[...] = jnp.maximum(jnp.abs(q_row - k_row), jnp.abs(q_col - k_col))
    index = lax.broadcasted_iota(jnp.int32, (1, padded), 1).astype(jnp.float32)
    h_row, h_col = jnp.full((1, padded), FAR, jnp.float32), jnp.full((1, padded), FAR, jnp.float32)
    for down, across, there, start, count, _ in strips:
        per = cols if across is None else R_MAX
        own = index - float(start)
        major = jnp.floor((own + 0.5) * (1.0 / per))
        minor = own - major * per
        row = major if down is None else major + pick(down, float(rows), float(-R_MAX))
        col = minor if across is None else minor + pick(across, float(cols), float(-R_MAX))
        if there is not True:
            row = row + jnp.where(there, 0.0, FAR)
        inside = jnp.logical_and(index >= float(start), index < float(start + count))
        h_row, h_col = jnp.where(inside, row, h_row), jnp.where(inside, col, h_col)
    far[...] = jnp.maximum(jnp.abs(q_row - h_row), jnp.abs(q_col - h_col))

    def own_part(h, _):
        radius = radii[h].astype(jnp.float32)
        score = dot3(split(q[:, lanes(h)]), split(k[:, lanes(h)]), ((1,), (1,))) * scale
        score = jnp.where(near[...] <= radius, score, EXCLUDED)
        highest = jnp.max(score, axis=1, keepdims=True)
        weight = jnp.exp(score - highest)
        top[h] = highest
        total[h] = jnp.sum(weight, axis=1, keepdims=True)
        acc[h] = dot3(split(weight), split(v[:, lanes(h)]), ((1,), (0,)))
        return 0

    lax.fori_loop(0, heads, own_part, 0)

    to_peer().wait_recv()
    passed[...] = state[pl.ds(parity * half, half)] + first[...]

    def receive():
        to_next().wait_recv()
        passed[...] = passed[...] + chain[...]

    pl.when(frame > 0)(receive)
    pl.when(frame < frames - 1)(lambda: to_next().start())
    for d in range(1, couples):
        to_alike(d).start()
    for h in range(2, heads):
        send_halo(h)

    def outer_part(h):
        await_halo(h)
        radius = radii[h].astype(jnp.float32)
        score = dot3(split(q[:, lanes(h)]), split(halo[h, 0]), ((1,), (1,))) * scale
        score = jnp.where(far[...] <= radius, score, EXCLUDED)
        highest = jnp.maximum(top[h], jnp.max(score, axis=1, keepdims=True))
        weight = jnp.exp(score - highest)
        fade = jnp.exp(top[h] - highest)
        below = total[h] * fade + jnp.sum(weight, axis=1, keepdims=True)
        above = acc[h] * fade + dot3(split(weight), split(halo[h, 1]), ((1,), (0,)))
        local[:, lanes(h)] = above / below

    def outer_step(h, _):
        outer_part(h)
        return 0

    lax.fori_loop(0, 2, outer_step, 0)

    mine = passed[...]
    for d in range(1, couples):
        to_alike(d).wait_recv()
        mine = mine + others[d - 1]
    full[pl.ds(parity * half, half)] = mine
    hand_back().start()

    pltpu.make_async_remote_copy(
        src_ref=full.at[pl.ds((1 - parity) * half, half)], dst_ref=full.at[pl.ds((1 - parity) * half, half)],
        send_sem=step_send.at[2], recv_sem=step_recv.at[2],
        device_id={"tile": peer}, device_id_type=MESH).wait_recv()

    seen = ((frame + 1) * (tiles * tokens)).astype(jnp.float32)

    def global_part(h, _):
        feature = jnp.maximum(q[:, lanes(h)], 0.0)
        numer = dot3(split(feature), split(full[h, 0:width, :]), ((1,), (0,))) * scale + full[h, width + 1:width + 2, :]
        denom = jnp.sum(feature * full[h, width:width + 1, :], axis=1, keepdims=True) * scale + seen
        glob[:, lanes(h)] = numer / denom
        return 0

    lax.fori_loop(0, heads, global_part, 0)
    lax.fori_loop(2, heads, outer_step, 0)

    for h in range(heads):
        for place, strip in enumerate(strips):
            guarded(strip[2], lambda place=place, h=h: halo_copy(place, h).wait_send())
    to_peer().wait_send()
    pl.when(frame < frames - 1)(lambda: to_next().wait_send())
    for d in range(1, couples):
        to_alike(d).wait_send()
    hand_back().wait_send()


def solution(mesh):
    frames, tiles = mesh.shape["block"], mesh.shape["tile"]
    grid_cols = min(4, tiles // 2)
    grid_rows = tiles // grid_cols

    def body(queries, keys, values, radii):
        rows, cols, dim = queries.shape[2:]
        heads = radii.shape[0]
        width = dim // heads
        tokens = rows * cols
        strips, used = strip_plan(rows, cols, grid_rows, grid_cols, 0, 0)
        padded = -(-used // 128) * 128
        half, depth, couples = heads // 2, width + 8, tiles // 2
        flat = [x.reshape(tokens, dim) for x in (queries, keys, values)]
        f32 = jnp.float32
        vmem = pl.BlockSpec(memory_space=pltpu.VMEM)
        local, glob = pl.pallas_call(
            functools.partial(kernel, (frames, tiles, grid_rows, grid_cols, rows, cols, heads, width)),
            out_shape=[jax.ShapeDtypeStruct((tokens, dim), f32)] * 2,
            in_specs=[pl.BlockSpec(memory_space=pltpu.SMEM), vmem, vmem, vmem],
            out_specs=[vmem, vmem],
            scratch_shapes=[
                pltpu.VMEM((heads, 2, padded, width), f32),
                pltpu.VMEM((heads, 2, padded, width), f32),
                pltpu.VMEM((tokens, tokens), f32),
                pltpu.VMEM((tokens, padded), f32),
                pltpu.VMEM((heads, tokens, width), f32),
                pltpu.VMEM((heads, tokens, 1), f32),
                pltpu.VMEM((heads, tokens, 1), f32),
                pltpu.VMEM((heads, depth, width), f32),
                pltpu.VMEM((heads, depth, width), f32),
                pltpu.VMEM((half, depth, width), f32),
                pltpu.VMEM((half, depth, width), f32),
                pltpu.VMEM((half, depth, width), f32),
                pltpu.VMEM((max(couples - 1, 1), half, depth, width), f32),
                pltpu.SemaphoreType.DMA((len(strips), heads)),
                pltpu.SemaphoreType.DMA((len(strips), heads)),
                pltpu.SemaphoreType.DMA((3,)),
                pltpu.SemaphoreType.DMA((3,)),
                pltpu.SemaphoreType.DMA((max(couples - 1, 1),)),
                pltpu.SemaphoreType.DMA((max(couples - 1, 1),)),
            ],
            compiler_params=pltpu.CompilerParams(
                collective_id=0, has_side_effects=True, vmem_limit_bytes=56 * 1024 * 1024
            ),
            cost_estimate=pl.CostEstimate(
                flops=2 * 3 * tokens * dim * 2 * (tokens + padded + width),
                bytes_accessed=5 * tokens * dim * 4,
                transcendentals=tokens * (tokens + padded) * heads,
            ),
        )(radii, *flat)
        return local.reshape(queries.shape), glob.reshape(queries.shape)

    spec = P(("groups", "block"), "tile", None, None, None)
    return jax.shard_map(
        body,
        mesh=mesh,
        in_specs=(spec, spec, spec, P()),
        out_specs=(spec, spec),
        check_vma=False,
    )
```

time: 246 us -> 99.7 us (0.41)
  waiting for transfers between devices: 119 us -> 0 us
  Pallas kernels: 0 us -> 94.9 us
  matrix products: 35.6 us -> 0 us
  local copies, waits for them, and re-layouts: 29.3 us -> 3.99 us
  blocking collectives: 22.6 us -> 0 us
  other arithmetic: 18.4 us -> 0 us
  between operations: 14.2 us -> 0.65 us
  starting transfers between devices: 3.96 us -> 0 us
    pallas_call x0 -> x1, Pallas kernels: none -> 94.9 us  [body(): pl.pallas_call(functools.partial(kernel, (frames, tiles, grid_rows, grid_...]
    ppermute x4 -> x0, waiting for transfers between devices: 94.4 us -> none  [from_behind(): return lax.ppermute(value, axis, pairs)]
    dot_general x5 -> x0, matrix products: 35.6 us -> none  [the longest x1 14.4 us: neighborhood(): jnp.einsum('hqk,khd->qhd', weights, value_rows, precision=lax.Precision.H...]
    psum x1 -> x0, waiting for transfers between devices: 25 us -> none  [body(): full_state, full_z, full_v = lax.psum(add_states(earlier, own), 'tile')]
    another operation x5 -> x0, local copies, waits for them, and re-layouts: 17.1 us -> none  [the longest x1 5.29 us: neighborhood(): value_rows = value_tile.reshape(key_h * key_w, head_count, head_dim)]
    all_gather x2 -> x0, blocking collectives: 12.5 us -> none  [entering(): everything = jax.tree.map(lambda part: lax.all_gather(part, axis), shard)]
    psum x1 -> x0, blocking collectives: 10 us -> none  [body(): full_state, full_z, full_v = lax.psum(add_states(earlier, own), 'tile')]
    select_n x9 -> x0, other arithmetic: 6.37 us -> none  [the longest x8 6.36 us: turn(): return jax.tree.map(lambda a, b: jnp.where(reached, a, b), new, before)]
  transfers between devices with their start and end apart: 6 -> 0, of which waited for: 5 -> 0; matrix products, arithmetic and copies ran while one was open for 22% -> 0% of each run, Pallas kernels for 0% -> 0%
where the time goes in v1:
time: 99.7 us; the launch traced here: 99.5 us
  Pallas kernels  94.9 us (95%)
  local copies, waits for them, and re-layouts  3.99 us (4%)
    pallas_call x1, Pallas kernels, body(): pl.pallas_call(functools.partial(kernel, (frames, tiles, grid_rows, grid_...  94.9 us
    unnamed x4, local copies, waits for them, and re-layouts  3.99 us

profile of v1, /device:TPU:19, one launch (start us, length us, event | category | flops | bytes accessed | tf_op | source)
XLA Modules:
  0.0 99.5 jit_solution(17223494274529666428)
XLA Ops:
  0.6 94.9 %shard_map.59 = (f32[384,1024]{1,0:T(8,128)}, f32[384,1024]{1,0:T(8,128)}) custom-call(s32[4]{0:T(128)} %radii.1, f32[384,1024]{1,0:T(8,128)} %bitcast.7, f32[384,1024]{1,0:T(8,128)} %bitcast.8, f32[384,1024]{1,0:T(8,128)} %bitcast.9), custom_call_target="tpu_custom_call" | custom-call | flops 4227858432 | bytes 7864320 | tf_op jit(solution)/shard_map/pallas_call | solution.py:337
  95.5 0.0 copy-start
  95.5 2.8 %copy.8 = f32[1,1,16,24,1024]{4,3,2,1,0:T(8,128)} copy(f32[1,1,16,24,1024]{4,3,2,1,0:T(8,128)} %bitcast.6) | data formatting | bytes 3145728
  98.4 0.0 copy-done
  98.4 1.1 %copy.9 = f32[1,1,16,24,1024]{4,3,2,1,0:T(8,128)} copy(f32[1,1,16,24,1024]{4,3,2,1,0:T(8,128)S(1)} %bitcast.5) | data formatting | bytes 3145728
Async XLA Ops:
  95.5 2.9 %copy-start = (f32[384,1024]{1,0:T(8,128)S(1)}, f32[384,1024]{1,0:T(8,128)}, u32[]{:S(2)}) copy-start(f32[384,1024]{1,0:T(8,128)} %get-tuple-element.5) | copy-start | bytes 4718596
